TPU v7x, 32 devices: a whole 2x2x4 slice. The times are simulated.
32 devices in a mesh: rows: 4 (over z), cols: 8 (over y, x, core).
Axes of the slice: x: 2, y: 2, z: 4, core: 2. Of those that a mesh axis runs over, the one named last changes fastest.
Arguments:
- momentum_prev: float32 [8192, 8192], P('rows', 'cols'), may hold values from -170 to 170
- gradient: bfloat16 [8192, 8192], P('rows', 'cols'), may hold values from -6 to 6
- q_prev: float32 [8192, 512], P('cols'), may hold values from -0.0625 to 0.0625
Outputs:
- momentum_next: float32 [8192, 8192], P('rows', 'cols')
- q_next: float32 [8192, 512], P('cols')
- update: bfloat16 [8192, 8192], P('rows', 'cols')
All inputs are finite; a program needn't handle non-finite values.
Results may differ from a plain program's by a relative error of at most 0.001.
Values sent between devices are 32-bit elements; how exact they have to be, the bound alone decides.
No kernel may reach another device: no remote copies, remote signals or barrier semaphores. Data moves between devices by JAX's collectives and lax.ppermute only.
A program may use at most 128 MiB of HBM per device.

v0:
```python
import jax
import jax.numpy as jnp
from jax import lax
from jax.sharding import PartitionSpec as P

D = 8192
RANK = 512


def body(momentum_prev, gradient, q_prev):
    highest = lax.Precision.HIGHEST
    momentum = 0.95 * momentum_prev + gradient.astype(jnp.float32)
    power_part = lax.psum_scatter(
        jnp.dot(momentum, q_prev, precision=highest, preferred_element_type=jnp.float32),
        "cols",
        scatter_dimension=0,
        tiled=True,
    )
    power = lax.all_gather(power_part, "cols", axis=0, tiled=True)
    partial_gram = jnp.dot(power.T, power, precision=highest, preferred_element_type=jnp.float32)
    raw_part = lax.dot_general(
        momentum,
        power,
        (((0,), (0,)), ((), ())),
        precision=highest,
        preferred_element_type=jnp.float32,
    )
    raw_cross, gram = lax.psum((raw_part, partial_gram), "rows")
    chol = jnp.linalg.cholesky(gram)
    basis = lax.linalg.triangular_solve(chol, power, left_side=False, lower=True, transpose_a=True)
    cross = lax.linalg.triangular_solve(
        chol, raw_cross, left_side=False, lower=True, transpose_a=True
    )
    col_sq = lax.psum(jnp.sum(cross * cross, axis=0), "cols")
    q_next = cross / (jnp.sqrt(col_sq) + 1e-08)
    momentum_next = momentum - 0.5 * lax.dot_general(
        basis,
        cross,
        (((1,), (1,)), ((), ())),
        precision=highest,
        preferred_element_type=jnp.float32,
    )
    factor = D / jnp.sqrt(jnp.float32(RANK))
    update = (
        factor
        * lax.dot_general(
            basis,
            q_next,
            (((1,), (1,)), ((), ())),
            precision=highest,
            preferred_element_type=jnp.float32,
        )
    ).astype(jnp.bfloat16)
    return (momentum_next, q_next, update)


def solution(mesh):
    in_specs = (P("rows", "cols"), P("rows", "cols"), P("cols", None))
    out_specs = (P("rows", "cols"), P("cols", None), P("rows", "cols"))
    return jax.shard_map(body, mesh=mesh, in_specs=in_specs, out_specs=out_specs, check_vma=False)
```

profile of v0, /device:TPU:0, one launch (start us, length us, event | category | flops | bytes accessed | tf_op | source)
XLA Modules:
  0.0 525.1 jit_solution(9703176806533271152)
XLA Ops:
  8.8 17.6 %fusion.10 = f32[2048,512]{1,0:T(8,128)} fusion(f32[1024,512]{1,0:T(8,128)S(1)} %copy-done, bf16[2048,1024]{1,0:T(8,128)(2,1)} %param.4, f32[2048,1024]{1,0:T(8,128)} %param.3), kind=kOutput, calls=%fused_computation.16 | convolution fusion | flops 12891193344 | bytes 18874368 | tf_op jit(solution)/shard_map/dot_general | solution.py:14
  26.4 54.1 %reduce-scatter.2.cloned.1.call-done = f32[256,512]{1,0:T(8,128)} async-done(((f32[2048,512]{1,0:T(8,128)}), f32[256,512]{1,0:T(8,128)}) %reduce-scatter.2.cloned.1.call-update) | async-done | bytes 524304 | tf_op jit(solution)/shard_map/reduce_scatter | solution.py:13
  80.6 38.7 %all-gather.2.cloned.1.call-done = f32[2048,512]{1,0:T(8,128)} async-done(((f32[256,512]{1,0:T(8,128)}), f32[2048,512]{1,0:T(8,128)}) %all-gather.2.cloned.1.call-update) | async-done | bytes 4194320 | tf_op jit(solution)/shard_map/all_gather | solution.py:19
  119.3 11.4 %fusion.63 = f32[512,512]{0,1:T(8,128)} fusion(f32[2048,512]{1,0:T(8,128)} %all-gather.2.cloned.1.call-done), kind=kOutput, calls=%fused_computation.103 | convolution fusion | flops 6442450944 | bytes 5242880 | tf_op jit(solution)/shard_map/dot_general | solution.py:20
  130.8 31.3 %fusion.9 = f32[1024,512]{1,0:T(8,128)} fusion(f32[2048,512]{1,0:T(8,128)} %all-gather.2.cloned.1.call-done, bf16[2048,1024]{1,0:T(8,128)(2,1)} %param.4, f32[2048,1024]{1,0:T(8,128)S(1)} %copy-done.1), kind=kOutput, calls=%fused_computation.15 | convolution fusion | flops 12891193344 | bytes 18874368 | tf_op jit(solution)/shard_map/dot_general | solution.py:21
  162.1 121.6 %all-reduce.4.cloned.1.call-done = (f32[512,512]{0,1:T(8,128)}, f32[1024,512]{1,0:T(8,128)}) async-done(((f32[512,512]{0,1:T(8,128)}, f32[1024,512]{1,0:T(8,128)}), (f32[512,512]{0,1:T(8,128)}, f32[1024,512]{1,0:T(8,128)})) %all-reduce.4.cloned.1.call-update) | async-done | bytes 3145744 | tf_op jit(solution)/shard_map/psum | solution.py:28
  287.7 11.7 %cholesky.104 = f32[128,128]{1,0:T(8,128)S(1)} custom-call(f32[128,128]{1,0:T(8,128)S(1)} %cholesky.266), custom_call_target="Cholesky" | custom-call | tf_op jit(solution)/shard_map/jit(cholesky)/cholesky | solution.py:29
  299.4 9.8 %custom-call.32 = f32[1,128,128]{1,2,0:T(8,128)S(1)} custom-call(f32[1,128,128]{2,1,0:T(8,128)S(1)} %get-tuple-element.35), custom_call_target="InvertDiagBlocksLowerTriangular" | custom-call | tf_op jit(solution)/shard_map/jit(cholesky)/cholesky | solution.py:29
  311.9 11.7 %cholesky.217 = f32[128,128]{1,0:T(8,128)S(1)} custom-call(f32[128,128]{1,0:T(8,128)S(1)} %cholesky.270), custom_call_target="Cholesky" | custom-call | tf_op jit(solution)/shard_map/jit(cholesky)/cholesky | solution.py:29
  323.7 10.0 %custom-call.33 = f32[1,128,128]{1,2,0:T(8,128)S(1)} custom-call(f32[1,128,128]{2,1,0:T(8,128)S(1)} %get-tuple-element.32), custom_call_target="InvertDiagBlocksLowerTriangular" | custom-call | tf_op jit(solution)/shard_map/jit(cholesky)/cholesky | solution.py:29
  335.2 11.7 %cholesky.238 = f32[128,128]{1,0:T(8,128)S(1)} custom-call(f32[128,128]{1,0:T(8,128)S(1)} %cholesky.275), custom_call_target="Cholesky" | custom-call | tf_op jit(solution)/shard_map/jit(cholesky)/cholesky | solution.py:29
  347.6 9.8 %custom-call.34 = f32[1,128,128]{1,2,0:T(8,128)S(1)} custom-call(f32[1,128,128]{2,1,0:T(8,128)S(1)} %get-tuple-element.29), custom_call_target="InvertDiagBlocksLowerTriangular" | custom-call | tf_op jit(solution)/shard_map/jit(cholesky)/cholesky | solution.py:29
  358.9 11.7 %cholesky.255 = f32[128,128]{1,0:T(8,128)S(1)} custom-call(f32[128,128]{1,0:T(8,128)S(1)} %convolution_subtract_fusion.6), custom_call_target="Cholesky" | custom-call | tf_op jit(solution)/shard_map/jit(cholesky)/cholesky | solution.py:29
  375.7 14.0 %while.1 = (s32[]{:T(128)}, f32[512,512]{1,0:T(8,128)}, s32[4,2]{0,1:T(2,128)S(1)}, f32[4,128,128]{2,1,0:T(8,128)}, s32[]{:T(128)}) while((s32[]{:T(128)}, f32[512,512]{1,0:T(8,128)}, s32[4,2]{0,1:T(2,128)S(1)}, f32[4,128,128]{2,1,0:T(8,128)}, s32[]{:T(128)}) %tuple.32), condition=%wide.while_cond, body=%wide.while_body.sunk | while | flops 2 | bytes 132205 | solution.py:30
  376.3 2.9 bitcast_dynamic-update-slice_fusion.2
  379.8 2.9 bitcast_dynamic-update-slice_fusion.2
  383.3 2.9 bitcast_dynamic-update-slice_fusion.2
  386.8 2.8 bitcast_dynamic-update-slice_fusion.2
  389.7 40.1 %custom-call.35 = f32[4,128,128]{1,2,0:T(8,128)S(1)} custom-call(f32[4,128,128]{2,1,0:T(8,128)} %get-tuple-element.10), custom_call_target="InvertDiagBlocksLowerTriangular" | custom-call | tf_op jit(solution)/shard_map/triangular_solve | solution.py:30
  429.8 1.8 fusion.29
  431.7 2.3 convolution_subtract_fusion.3
  434.6 2.9 convolution_subtract_fusion.2
  438.1 3.9 fusion.20
  443.7 14.0 %psum.23 = f32[512]{0:T(512)S(1)} all-reduce(f32[512]{0:T(512)S(1)} %multiply_reduce_fusion), channel_id=1, replica_groups=mesh['rows'=4,'cols'=8] {'cols'}, use_global_device_ids=true, to_apply=%region_12.13 | all-reduce | flops 512 | bytes 4096 | tf_op jit(solution)/shard_map/psum | solution.py:34
  457.7 2.5 fusion.23
  460.2 3.1 convolution_subtract_fusion.1
  464.4 4.6 convolution_subtract_fusion
  470.1 6.9 %fusion.6 = f32[2048,128]{1,0:T(8,128)S(1)} fusion(f32[2048,128]{0,1:T(8,128)S(1)} %fusion.49, f32[2048,128]{0,1:T(8,128)S(1)} %fusion.47, f32[2048,128]{0,1:T(8,128)S(1)} %fusion.23, f32[2048,512]{1,0:T(8,128)S(1)} %copy-done.2, f32[512,512]{1,0:T(8,128)} %get-tuple-element.95), kind=kOutput, calls=%fused_computation.12 | convolution fusion | flops 1209794560 | bytes 5439488 | tf_op jit(solution)/shard_map/triangular_solve | solution.py:30
  477.0 2.1 fusion.51
  480.6 2.9 copy.8
  483.6 17.0 %multiply_convert_fusion = bf16[2048,1024]{1,0:T(8,128)(2,1)} fusion(f32[1024,512]{0,1:T(8,128)} %broadcast_divide_fusion, f32[2048,128]{0,1:T(8,128)} %fusion.51, f32[2048,128]{0,1:T(8,128)} %copy-done.15, f32[2048,128]{0,1:T(8,128)} %copy-done.10, f32[2048,128]{0,1:T(8,128)S(1)} %fusion.23), kind=kOutput, calls=%fused_computation.2 | convolution fusion | flops 12892241920 | bytes 10485760 | tf_op jit(solution)/shard_map/dot_general | solution.py:46
  500.7 17.7 %multiply_subtract_fusion = f32[2048,1024]{1,0:T(8,128)} fusion(f32[2048,128]{0,1:T(8,128)S(1)} %copy-done.20, f32[2048,128]{0,1:T(8,128)S(1)} %copy-done.16, f32[2048,128]{0,1:T(8,128)S(1)} %copy-done.11, f32[2048,128]{0,1:T(8,128)S(1)} %fusion.23, bf16[2048,1024]{1,0:T(8,128)(2,1)S(1)} %copy-done.3, f32[2048,1024]{1,0:T(8,128)} %param.3, ...), kind=kOutput, calls=%fused_computation.3 | convolution fusion | flops 12900106240 | bytes 27262976 | tf_op jit(solution)/shard_map/dot_general | solution.py:36
  (91 shorter events, 23.8 us)
Async XLA Ops:
  7.2 1.6 copy-start
  7.2 73.4 %reduce-scatter.2.cloned.1.call-start = ((), (), s32[]{:S(2)}) async-start(), calls=%async_computation.1 | async-start | bytes 4718592 | tf_op jit(solution)/shard_map/reduce_scatter | solution.py:13
  26.4 93.0 %all-gather.2.cloned.1.call-start = ((), (), s32[]{:S(2)}) async-start(), calls=%async_computation.2 | async-start | bytes 4718592 | tf_op jit(solution)/shard_map/all_gather | solution.py:19
  80.6 203.1 %all-reduce.4.cloned.1.call-start = ((), (), s32[]{:S(2)}) async-start(), calls=%async_computation.3 | async-start | bytes 6291456 | tf_op jit(solution)/shard_map/psum | solution.py:28
  119.3 11.4 %copy-start.1 = (f32[2048,1024]{1,0:T(8,128)S(1)}, f32[2048,1024]{1,0:T(8,128)}, u32[]{:S(2)}) copy-start(f32[2048,1024]{1,0:T(8,128)} %param.3) | copy-start | bytes 25165828
  286.7 1.0 copy-start.21
  429.8 4.7 copy-start.22
  431.6 11.0 %copy-start.4 = (f32[1024,128]{0,1:T(8,128)}, f32[1024,128]{0,1:T(8,128)S(1)}, u32[]{:S(2)}) copy-start(f32[1024,128]{0,1:T(8,128)S(1)} %fusion.29) | copy-start | bytes 1572868
  434.6 8.1 %copy-start.7 = (f32[1024,128]{0,1:T(8,128)}, f32[1024,128]{0,1:T(8,128)S(1)}, u32[]{:S(2)}) copy-start(f32[1024,128]{0,1:T(8,128)S(1)} %fusion.46) | copy-start | bytes 1572868
  438.1 4.6 copy-start.12
  442.7 0.8 copy-start.17
  457.7 6.7 %copy-start.2 = (f32[2048,512]{1,0:T(8,128)S(1)}, f32[2048,512]{1,0:T(8,128)}, u32[]{:S(2)}) copy-start(f32[2048,512]{1,0:T(8,128)} %all-gather.2.cloned.1.call-done) | copy-start | bytes 12582916
  464.4 12.6 %copy-start.10 = (f32[2048,128]{0,1:T(8,128)}, f32[2048,128]{0,1:T(8,128)S(1)}, u32[]{:S(2)}) copy-start(f32[2048,128]{0,1:T(8,128)S(1)} %fusion.47) | copy-start | bytes 3145732
  470.1 9.0 %copy-start.15 = (f32[2048,128]{0,1:T(8,128)}, f32[2048,128]{0,1:T(8,128)S(1)}, u32[]{:S(2)}) copy-start(f32[2048,128]{0,1:T(8,128)S(1)} %fusion.49) | copy-start | bytes 3145732
  470.1 9.0 %copy-start.5 = (f32[1024,128]{0,1:T(8,128)S(1)}, f32[1024,128]{0,1:T(8,128)}, u32[]{:S(2)}) copy-start(f32[1024,128]{0,1:T(8,128)} %copy-done.4) | copy-start | bytes 1572868
  470.1 9.0 %copy-start.8 = (f32[1024,128]{0,1:T(8,128)S(1)}, f32[1024,128]{0,1:T(8,128)}, u32[]{:S(2)}) copy-start(f32[1024,128]{0,1:T(8,128)} %copy-done.7) | copy-start | bytes 1572868
  470.1 9.0 %copy-start.13 = (f32[1024,128]{0,1:T(8,128)S(1)}, f32[1024,128]{0,1:T(8,128)}, u32[]{:S(2)}) copy-start(f32[1024,128]{0,1:T(8,128)} %copy-done.12) | copy-start | bytes 1572868
  470.1 9.0 %copy-start.18 = (f32[1024,128]{0,1:T(8,128)S(1)}, f32[1024,128]{0,1:T(8,128)}, u32[]{:S(2)}) copy-start(f32[1024,128]{0,1:T(8,128)} %copy-done.17) | copy-start | bytes 1572868
  483.5 17.1 %copy-start.3 = (bf16[2048,1024]{1,0:T(8,128)(2,1)S(1)}, bf16[2048,1024]{1,0:T(8,128)(2,1)}, u32[]{:S(2)}) copy-start(bf16[2048,1024]{1,0:T(8,128)(2,1)} %param.4) | copy-start | bytes 12582916
  483.5 17.1 %copy-start.6 = (f32[1024,128]{0,1:T(8,128)S(1)}, f32[1024,128]{0,1:T(8,128)}, u32[]{:S(2)}) copy-start(f32[1024,128]{0,1:T(8,128)} %copy-done.4) | copy-start | bytes 1572868
  483.5 17.1 %copy-start.9 = (f32[1024,128]{0,1:T(8,128)S(1)}, f32[1024,128]{0,1:T(8,128)}, u32[]{:S(2)}) copy-start(f32[1024,128]{0,1:T(8,128)} %copy-done.7) | copy-start | bytes 1572868
  483.5 17.1 %copy-start.11 = (f32[2048,128]{0,1:T(8,128)S(1)}, f32[2048,128]{0,1:T(8,128)}, u32[]{:S(2)}) copy-start(f32[2048,128]{0,1:T(8,128)} %copy-done.10) | copy-start | bytes 3145732
  483.5 17.1 %copy-start.14 = (f32[1024,128]{0,1:T(8,128)S(1)}, f32[1024,128]{0,1:T(8,128)}, u32[]{:S(2)}) copy-start(f32[1024,128]{0,1:T(8,128)} %copy-done.12) | copy-start | bytes 1572868
  483.5 17.1 %copy-start.16 = (f32[2048,128]{0,1:T(8,128)S(1)}, f32[2048,128]{0,1:T(8,128)}, u32[]{:S(2)}) copy-start(f32[2048,128]{0,1:T(8,128)} %copy-done.15) | copy-start | bytes 3145732
  483.6 17.1 %copy-start.19 = (f32[1024,128]{0,1:T(8,128)S(1)}, f32[1024,128]{0,1:T(8,128)}, u32[]{:S(2)}) copy-start(f32[1024,128]{0,1:T(8,128)} %copy-done.17) | copy-start | bytes 1572868
  483.6 17.1 %copy-start.20 = (f32[2048,128]{0,1:T(8,128)S(1)}, f32[2048,128]{0,1:T(8,128)}, u32[]{:S(2)}) copy-start(f32[2048,128]{0,1:T(8,128)} %fusion.51) | copy-start | bytes 3145732
Sparse Core Ops, SparseCore 0:
  26.5 53.9 reduce-scatter.1
  82.6 36.7 all-gather.1
  162.2 121.4 all-reduce.3
where the time goes:
time: 532 us; the launch traced here: 525 us
  waiting for transfers between devices  214 us (40%)
  matrix products  135 us (25%)
  other arithmetic  123 us (23%)
  local copies, waits for them, and re-layouts  22 us (4%)
  between operations  16.9 us (3%)
  blocking collectives  14 us (3%)
    psum x1, waiting for transfers between devices, body(): raw_cross, gram = lax.psum((raw_part, partial_gram), 'rows')  122 us
    another operation x14, other arithmetic, body(): chol = jnp.linalg.cholesky(gram)  78.5 us
    reduce_scatter x1, waiting for transfers between devices, body(): lax.psum_scatter(jnp.dot(momentum, q_prev, precision=highest, preferred_e...  54.1 us
    another operation x3, other arithmetic, body(): lax.linalg.triangular_solve(chol, power, left_side=False, lower=True, tra...  41.4 us
    all_gather x1, waiting for transfers between devices, body(): power = lax.all_gather(power_part, 'cols', axis=0, tiled=True)  38.7 us
    dot_general x1, matrix products, body(): lax.dot_general(momentum, power, (((0,), (0,)), ((), ())), precision=high...  31.3 us
    another operation x7, matrix products, body(): lax.linalg.triangular_solve(chol, power, left_side=False, lower=True, tra...  21.2 us
    dot_general x1, matrix products, body(): lax.dot_general(basis, cross, (((1,), (1,)), ((), ())), precision=highest...  17.7 us
  transfers between devices with their start and end apart: 3, of which 3 were waited for; matrix products, arithmetic and copies ran while one was open for 0% of the time, Pallas kernels for 0%

commit v1 on v0

v1 whole, which is shorter than its diff:
```python
import functools

import jax
import jax.numpy as jnp
from jax import lax
from jax.experimental import pallas as pl
from jax.experimental.pallas import tpu as pltpu
from jax.sharding import PartitionSpec as P

CHUNK = 128
PANEL = 8
F32, BF16 = jnp.float32, jnp.bfloat16
HIGHEST = lax.Precision.HIGHEST
NN = (((1,), (0,)), ((), ()))
NT = (((1,), (1,)), ((), ()))
MIB = 1024 * 1024
VMEM = pl.BlockSpec(memory_space=pltpu.VMEM)
SMEM = pl.BlockSpec(memory_space=pltpu.SMEM)
HBM = pl.BlockSpec(memory_space=pltpu.HBM)
DMA = pltpu.SemaphoreType.DMA


def params(mib):
    return pltpu.CompilerParams(vmem_limit_bytes=mib * MIB)


def shape(dims, dtype=F32):
    return jax.ShapeDtypeStruct(dims, dtype)


def cost(flops, nbytes):
    return pl.CostEstimate(flops=int(flops), bytes_accessed=int(nbytes), transcendentals=0)


def split(x):
    hi = x.astype(BF16)
    return hi, (x - hi.astype(F32)).astype(BF16)


def dot1(a, b, dims):
    return lax.dot_general(a, b, dims, preferred_element_type=F32)


def dot3(ah, al, bh, bl, dims=NN):
    return dot1(ah, bh, dims) + (dot1(al, bh, dims) + dot1(ah, bl, dims))


def dot_high(a, b, dims):
    return lax.dot_general(a, b, dims, precision=HIGHEST, preferred_element_type=F32)


def bit_orders(bits):
    rest = list(range(1, bits))
    half = (len(rest) + 1) // 2
    return rest, rest[half:] + rest[:half]


def position_masks(bits, parity):
    orders = bit_orders(bits)

    def walk(order):
        masks = [0]
        for bit in reversed(order):
            masks = masks + [m ^ (1 << bit) for m in masks]
        return masks

    return walk(orders[parity]) + [1 ^ m for m in walk(orders[1 - parity])]


def pair_perms(bits):
    orders = bit_orders(bits)
    n = 1 << bits
    return [[(j, j ^ (1 << orders[j & 1][step])) for j in range(n)] for step in range(bits - 1)]


def after(x, token):
    return lax.optimization_barrier((x, token))[0]


def gather_by_pairs(x, n, axis):
    own = [x] + [lax.ppermute(x, axis, [(j, j ^ m) for j in range(n)]) for m in range(2, n, 2)]
    return own, lax.ppermute(jnp.concatenate(own, axis=0), axis, [(j, j ^ 1) for j in range(n)])


def line_all_reduce(parts, axis, n):
    me = lax.axis_index(axis)
    half = n // 2
    done = []
    for x in parts:
        for s in range(half - 1):
            x = x + lax.ppermute(x, axis, [(s, s + 1), (n - 1 - s, n - 2 - s)])
        x = x + lax.ppermute(x, axis, [(half - 1, half), (half, half - 1)])
        for s in reversed(range(half - 1)):
            r = lax.ppermute(x, axis, [(s + 1, s), (n - 2 - s, n - 1 - s)])
            x = jnp.where((me == s) | (me == n - 1 - s), r, x)
        done.append(x)
    return done


def row_copies(order_ref, src, dst, sems, block):
    out = []
    for t in range(dst.shape[0]):
        rows = pl.ds(pl.multiple_of(order_ref[t] * block, block), block)
        out.append(pltpu.make_async_copy(src.at[rows, :], dst.at[t], sems.at[t]))
        out[-1].start()
    return out


def store_parts(p, t, half, widths, keep, send):
    off = 0
    for g, w in enumerate(widths):
        piece = p[:, off : off + w].T
        if t < half:
            keep[g][t] = piece
        else:
            send[g][t - half] = piece
        off += w


def first_kernel(widths, order_ref, mp_ref, g_ref, q_ref, hi_ref, lo_ref, keep_ref, send_ref, mb, gb, qb, sm, sg, sq):
    blocks, block, _ = mb.shape
    width = widths[0]
    q_copy = pltpu.make_async_copy(q_ref, qb, sq)
    q_copy.start()
    g_copies = row_copies(order_ref, g_ref, gb, sg, block)
    m_copies = row_copies(order_ref, mp_ref, mb, sm, block)
    q_copy.wait()
    qh, ql = split(qb[:, :width])
    for t in range(blocks):
        g_copies[t].wait()
        m_copies[t].wait()
        h, l = split(0.95 * mb[t] + gb[t].astype(F32))
        rows = slice(t * block, (t + 1) * block)
        hi_ref[rows, :] = h
        lo_ref[rows, :] = l
        both = dot1(h, jnp.concatenate([qh, ql], axis=1), NN)
        p = both[:, :width] + (both[:, width:] + dot1(l, qh, NN))
        store_parts(p, t, blocks // 2, widths, [keep_ref], [send_ref])


def first_call(order, mp, g, q, width, blocks):
    rows, cols = mp.shape
    block, half = rows // blocks, blocks // 2
    return pl.pallas_call(
        functools.partial(first_kernel, [width]),
        in_specs=[SMEM, HBM, HBM, HBM],
        out_specs=[VMEM] * 4,
        out_shape=[shape((rows, cols), BF16)] * 2 + [shape((half, width, block))] * 2,
        scratch_shapes=[
            pltpu.VMEM((blocks, block, cols), F32),
            pltpu.VMEM((blocks, block, cols), BF16),
            pltpu.VMEM(q.shape, F32),
            DMA((blocks,)),
            DMA((blocks,)),
            DMA,
        ],
        compiler_params=params(32),
        cost_estimate=cost(6 * rows * cols * width, 6 * rows * cols),
        name="momentum_and_power",
    )(order, mp, g, q)


def rest_kernel(widths, first, hi_ref, lo_ref, q_ref, *refs):
    n = len(widths)
    keep, send, (qb, sem) = refs[:n], refs[n : 2 * n], refs[2 * n :]
    half, _, block = keep[0].shape
    copy = pltpu.make_async_copy(q_ref, qb, sem)
    copy.start()
    copy.wait()
    qh, ql = split(qb[:, first:])
    for t in range(2 * half):
        rows = slice(t * block, (t + 1) * block)
        store_parts(dot3(hi_ref[rows, :], lo_ref[rows, :], qh, ql), t, half, widths, keep, send)


def rest_call(hi, lo, q, widths, blocks):
    rows, cols = hi.shape
    block, half = rows // blocks, blocks // 2
    width = sum(widths)
    out = pl.pallas_call(
        functools.partial(rest_kernel, widths, q.shape[1] - width),
        in_specs=[VMEM, VMEM, HBM],
        out_specs=[VMEM] * (2 * len(widths)),
        out_shape=[shape((half, w, block)) for w in widths] * 2,
        scratch_shapes=[pltpu.VMEM(q.shape, F32), DMA],
        compiler_params=params(16),
        cost_estimate=cost(6 * rows * cols * width, 4 * rows * cols),
        name="power",
    )(hi, lo, q)
    return out[: len(widths)], out[len(widths) :]


def raw_kernel(pa_ref, pb_ref, hi_ref, lo_ref, *refs):
    outs, acc = refs[:-1], refs[-1]
    half, width, block = pa_ref.shape
    for t in range(2 * half):
        ph, plo = split(pa_ref[t] if t < half else pb_ref[t - half])
        rows = slice(t * block, (t + 1) * block)
        both = dot1(jnp.concatenate([ph, plo], axis=0), hi_ref[rows, :], NN)
        term = both[:width] + (both[width:] + dot1(ph, lo_ref[rows, :], NN))
        acc[...] = term if t == 0 else acc[...] + term
    off = 0
    for out in outs:
        out[...] = acc[off : off + out.shape[0]]
        off += out.shape[0]


def raw_call(pa, pb, hi, lo, parts):
    rows, cols = hi.shape
    width = pa.shape[1]
    return pl.pallas_call(
        raw_kernel,
        in_specs=[VMEM] * 4,
        out_specs=[VMEM] * len(parts),
        out_shape=[shape((p, cols)) for p in parts],
        scratch_shapes=[pltpu.VMEM((width, cols), F32)],
        compiler_params=params(16),
        cost_estimate=cost(6 * rows * cols * width, 4 * rows * cols),
        name="raw",
    )(pa, pb, hi, lo)


def gram_kernel(skip, me_ref, *refs):
    pieces, out_ref = refs[:-1], refs[-1]
    half = pieces[0].shape[0]
    slice_rows = CHUNK // (2 * half)
    start = me_ref[0] * slice_rows
    groups = list(zip(pieces[::2], pieces[1::2]))
    sums = [None] * len(groups)
    for t in range(2 * half):
        part = [pair[t // half].at[t % half] for pair in groups]
        mine = []
        off = 0
        for ref in part:
            for c in range(0, ref.shape[0], CHUNK):
                if off + c >= skip:
                    mine.append(ref[pl.ds(pl.multiple_of(c + start, slice_rows), slice_rows), :])
            off += ref.shape[0]
        mine = jnp.concatenate(mine, axis=0)
        for d, ref in enumerate(part):
            term = dot_high(ref[...], mine, NT)
            sums[d] = term if sums[d] is None else sums[d] + term
    off = 0
    for s in sums:
        out_ref[:, off : off + s.shape[0]] = s.T
        off += s.shape[0]


def gram_call(me, parts, skip):
    refs = [x for pair in parts for x in pair]
    half, _, block = refs[0].shape
    size = sum(pair[0].shape[1] for pair in parts)
    rows = (size - skip) // (2 * half)
    return pl.pallas_call(
        functools.partial(gram_kernel, skip),
        in_specs=[SMEM] + [VMEM] * len(refs),
        out_specs=VMEM,
        out_shape=shape((rows, size)),
        compiler_params=params(16),
        cost_estimate=cost(4e9, 8 * len(refs) * half * block * CHUNK),
        name="gram",
    )(me, *refs)


def eliminate(s_ref, w_ref):
    n = s_ref.shape[0]
    row = lax.broadcasted_iota(jnp.int32, (n, n), 0)
    col = lax.broadcasted_iota(jnp.int32, (n, n), 1)
    w_ref[...] = (row == col).astype(F32)
    full = (PANEL, n)
    sub = lax.broadcasted_iota(jnp.int32, full, 0)
    for base in range(0, n, PANEL):
        panel = s_ref[base : base + PANEL, :]
        wpanel = w_ref[base : base + PANEL, :]
        rows = [jnp.broadcast_to(panel[i : i + 1, :], full) for i in range(PANEL)]
        wrows = [jnp.broadcast_to(wpanel[i : i + 1, :], full) for i in range(PANEL)]
        v = {}
        for i in range(PANEL):
            for k in range(i, PANEL):
                v[i, k] = jnp.broadcast_to(rows[i][:, base + k : base + k + 1], full)
        mult, inv = {}, []
        for i in range(PANEL):
            r = 1.0 / v[i, i]
            inv.append(r)
            for a in range(i + 1, PANEL):
                m = v[i, a] * r
                mult[i, a] = m
                for k in range(a, PANEL):
                    v[a, k] = v[a, k] - m * v[i, k]
                rows[a] = rows[a] - m * rows[i]
                wrows[a] = wrows[a] - m * wrows[i]
        out = wrows[0] * lax.rsqrt(v[0, 0])
        for i in range(1, PANEL):
            out = jnp.where(sub == i, wrows[i] * lax.rsqrt(v[i, i]), out)
        w_ref[base : base + PANEL, :] = out
        for below in range(base + PANEL, n, PANEL):
            s = s_ref[below : below + PANEL, :]
            w = w_ref[below : below + PANEL, :]
            f = [jnp.broadcast_to(s[:, base + i : base + i + 1], full) for i in range(PANEL)]
            for i in range(PANEL):
                for a in range(i + 1, PANEL):
                    f[a] = f[a] - mult[i, a] * f[i]
            for i in range(PANEL):
                g = f[i] * inv[i]
                s = s - g * rows[i]
                w = w - g * wrows[i]
            s_ref[below : below + PANEL, :] = s
            w_ref[below : below + PANEL, :] = w


def chol_kernel(n_own, skip, order_ref, *refs):
    own, other = refs[:n_own], refs[n_own]
    prev = refs[n_own + 1] if skip else None
    out_ref, g_ref, s_ref, w_ref = refs[n_own + (2 if skip else 1) :]
    size = out_ref.shape[0]
    rows = own[0].shape[0]
    slice_rows = CHUNK // (2 * n_own)
    for i in range(2 * n_own):
        start = order_ref[i] * slice_rows
        for c in range(rows // slice_rows):
            at = c * slice_rows
            if i < n_own:
                piece = own[i][at : at + slice_rows, :]
            else:
                at += (i - n_own) * rows
                piece = other[at : at + slice_rows, :]
            g_ref[pl.ds(pl.multiple_of(c * CHUNK + start, slice_rows), slice_rows), :] = piece
    if skip:
        out_ref[:skip, :skip] = prev[...]
    for base in range(skip, size, CHUNK):
        here = slice(base, base + CHUNK)
        grow = slice(base - skip, base - skip + CHUNK)
        s = g_ref[grow, here]
        if base:
            before = out_ref[:base, :base]
            lrow = dot_high(g_ref[grow, :base], before, NT)
            s = s - dot_high(lrow, lrow, NT)
        s_ref[...] = s
        eliminate(s_ref, w_ref)
        w = w_ref[...]
        out_ref[here, here] = w
        if base:
            out_ref[:base, here] = jnp.zeros((base, CHUNK), F32)
            out_ref[here, :base] = -dot_high(w, dot_high(lrow, before, NN), NN)


def chol_call(order, own, other, prev, skip):
    size = own[0].shape[1]
    args = list(own) + [other] + ([prev] if skip else [])
    return pl.pallas_call(
        functools.partial(chol_kernel, len(own), skip),
        in_specs=[SMEM] + [VMEM] * len(args),
        out_specs=VMEM,
        out_shape=shape((size, size)),
        scratch_shapes=[pltpu.VMEM((size - skip, size), F32)] + [pltpu.VMEM((CHUNK, CHUNK), F32)] * 2,
        compiler_params=params(16),
        cost_estimate=cost(6e9 * (size - skip) / CHUNK, 8 * size * size),
        name="chol",
    )(order, *args)


def basis_kernel(inv_ref, *refs):
    pieces, (bh_ref, bl_ref) = refs[:-2], refs[-2:]
    half, _, block = pieces[0].shape
    ih, il = split(inv_ref[...])
    for t in range(2 * half):
        pt = jnp.concatenate([p[t % half] for p in pieces[t // half :: 2]], axis=0)
        ph, plo = split(pt)
        rows = slice(t * block, (t + 1) * block)
        bh_ref[rows, :], bl_ref[rows, :] = split(dot3(ih, il, ph, plo).T)


def basis_call(inv, parts):
    refs = [x for pair in parts for x in pair]
    half, _, block = refs[0].shape
    rank = inv.shape[0]
    return pl.pallas_call(
        basis_kernel,
        in_specs=[VMEM] * (1 + len(refs)),
        out_specs=[VMEM, VMEM],
        out_shape=[shape((2 * half * block, rank), BF16)] * 2,
        compiler_params=params(16),
        cost_estimate=cost(12 * rank * rank * block * half, 16 * rank * block * half),
        name="basis",
    )(inv, *refs)


def cross_kernel(skip, inv_ref, *refs):
    raws, (out_ref, ch_ref, cl_ref, sq_ref) = refs[:-4], refs[-4:]
    size = skip + out_ref.shape[0]
    ih, il = split(inv_ref[skip:size, :size])
    rh, rl = split(jnp.concatenate([r[...] for r in raws], axis=0))
    cross = dot3(ih, il, rh, rl)
    out_ref[...] = cross
    ch_ref[...], cl_ref[...] = split(cross)
    sq_ref[...] = jnp.sum(cross * cross, axis=1, keepdims=True).T


def cross_call(inv, raws, skip):
    cols = raws[0].shape[1]
    rows = sum(r.shape[0] for r in raws) - skip
    return pl.pallas_call(
        functools.partial(cross_kernel, skip),
        in_specs=[VMEM] * (1 + len(raws)),
        out_specs=[VMEM] * 4,
        out_shape=[shape((rows, cols)), shape((rows, cols), BF16), shape((rows, cols), BF16), shape((1, rows))],
        compiler_params=params(16),
        cost_estimate=cost(6 * rows * (rows + skip) * cols, 8 * rows * cols),
        name="cross",
    )(inv, *raws)


def store_rows(order_ref, t, buf, out_ref, sem):
    block = buf.shape[1]
    rows = pl.ds(pl.multiple_of(order_ref[t] * block, block), block)
    copy = pltpu.make_async_copy(buf.at[t], out_ref.at[rows, :], sem.at[t])
    copy.start()
    return copy


def momentum_kernel(n, order_ref, bh_ref, bl_ref, hi_ref, lo_ref, *refs):
    ch_refs, cl_refs, (out_ref, ch, cl, buf, sem) = refs[:n], refs[n : 2 * n], refs[2 * n :]
    blocks, block, _ = buf.shape
    off = 0
    for a, b in zip(ch_refs, cl_refs):
        ch[off : off + a.shape[0], :] = a[...]
        cl[off : off + a.shape[0], :] = b[...]
        off += a.shape[0]
    copies = []
    for t in range(blocks):
        rows = slice(t * block, (t + 1) * block)
        prod = dot3(bh_ref[rows, :], bl_ref[rows, :], ch[...], cl[...])
        buf[t] = (hi_ref[rows, :].astype(F32) + lo_ref[rows, :].astype(F32)) - 0.5 * prod
        copies.append(store_rows(order_ref, t, buf, out_ref, sem))
    for copy in copies:
        copy.wait()


def momentum_call(order, bh, bl, hi, lo, chs, cls):
    rows, cols = hi.shape
    rank, blocks = bh.shape[1], order.shape[0]
    return pl.pallas_call(
        functools.partial(momentum_kernel, len(chs)),
        in_specs=[SMEM] + [VMEM] * (4 + 2 * len(chs)),
        out_specs=HBM,
        out_shape=shape((rows, cols)),
        scratch_shapes=[pltpu.VMEM((rank, cols), BF16)] * 2 + [pltpu.VMEM((blocks, rows // blocks, cols), F32), DMA((blocks,))],
        compiler_params=params(16),
        cost_estimate=cost(6 * rows * cols * rank, 8 * rows * cols),
        name="momentum_next",
    )(order, bh, bl, hi, lo, *chs, *cls)


def update_kernel(n, factor, order_ref, bh_ref, bl_ref, *refs):
    crosses, sqs = refs[:n], refs[n : 2 * n]
    out_ref, qn_ref, ch, cl, qt, buf, qbuf, sem, qsem = refs[2 * n :]
    blocks, block, cols = buf.shape
    off = 0
    for c, sq in zip(crosses, sqs):
        size = c.shape[0]
        scale = jnp.broadcast_to(1.0 / (jnp.sqrt(sq[...]) + 1e-08), (CHUNK, size)).T[:, :1]
        q = c[...] * scale
        qt[off : off + size, :] = q
        ch[off : off + size, :], cl[off : off + size, :] = split(q)
        off += size
    copies = []
    step = cols // blocks
    for t in range(blocks):
        rows = slice(t * block, (t + 1) * block)
        prod = dot3(bh_ref[rows, :], bl_ref[rows, :], ch[...], cl[...])
        buf[t] = (factor * prod).astype(BF16)
        copies.append(store_rows(order_ref, t, buf, out_ref, sem))
        qbuf[t] = qt[:, t * step : (t + 1) * step].T
        copy = pltpu.make_async_copy(qbuf.at[t], qn_ref.at[pl.ds(t * step, step), :], qsem.at[t])
        copy.start()
        copies.append(copy)
    for copy in copies:
        copy.wait()


def update_call(order, bh, bl, crosses, sqs, factor):
    rows, rank = bh.shape
    cols, blocks = crosses[0].shape[1], order.shape[0]
    return pl.pallas_call(
        functools.partial(update_kernel, len(crosses), factor),
        in_specs=[SMEM] + [VMEM] * (2 + 2 * len(crosses)),
        out_specs=[HBM, HBM],
        out_shape=[shape((rows, cols), BF16), shape((cols, rank))],
        scratch_shapes=[pltpu.VMEM((rank, cols), BF16)] * 2
        + [
            pltpu.VMEM((rank, cols), F32),
            pltpu.VMEM((blocks, rows // blocks, cols), BF16),
            pltpu.VMEM((blocks, cols // blocks, rank), F32),
            DMA((blocks,)),
            DMA((blocks,)),
        ],
        compiler_params=params(16),
        cost_estimate=cost(6 * rows * cols * rank, 8 * rows * cols),
        name="update",
    )(order, bh, bl, *crosses, *sqs)


def plan(chunks):
    if chunks < 4:
        return [CHUNK] * chunks, [[CHUNK]] * chunks, [chunks - 1]
    last = (chunks - 2) * CHUNK
    groups = [CHUNK, CHUNK, last]
    return groups, [[CHUNK], [CHUNK], [last - CHUNK, CHUNK // 2, CHUNK // 2]], [1, 2]


def fast(n_rows, n_cols, momentum_prev, gradient, q_prev):
    rank = q_prev.shape[1]
    widths, line_parts, ends = plan(rank // CHUNK)
    bits = n_cols.bit_length() - 1
    me = lax.axis_index("cols").astype(jnp.int32)
    masks = jnp.where(
        me % 2 == 0,
        jnp.array(position_masks(bits, 0), jnp.int32),
        jnp.array(position_masks(bits, 1), jnp.int32),
    )
    order = me ^ masks
    parity_order = me ^ jnp.array(list(range(0, n_cols, 2)) + list(range(1, n_cols, 2)), jnp.int32)
    core = [(j, j ^ 1) for j in range(n_cols)]
    perms = pair_perms(bits)

    hi, lo, keep, send = first_call(order, momentum_prev, gradient, q_prev, widths[0], n_cols)
    keep, send = [keep], [send]
    if len(widths) > 1:
        k, s = rest_call(hi, lo, q_prev, widths[1:], n_cols)
        keep, send = keep + list(k), send + list(s)
    parts, raws, inv, skip, crosses = [], [], None, 0, []
    token = None
    for g, width in enumerate(widths):
        k, r = keep[g], lax.ppermute(send[g], "cols", core)
        if token is not None:
            r = after(r, token)
        for perm in perms:
            n = k.shape[0] // 2
            s = lax.ppermute(k[n:] + r[n:], "cols", perm)
            k, r = k[:n] + r[:n], s
        x = token = k + r
        for perm in reversed(perms):
            x = jnp.concatenate([x, lax.ppermute(x, "cols", perm)], axis=0)
        parts.append((x, lax.ppermute(x, "cols", core)))
    done = 0
    for end in ends:
        gram = gram_call(me.reshape(1), parts[: end + 1], skip)
        across = [gram] + [lax.ppermute(gram, "rows", [(i, i ^ m) for i in range(n_rows)]) for m in range(1, n_rows)]
        while len(across) > 1:
            across = [a + b for a, b in zip(across[::2], across[1::2])]
        own, other = gather_by_pairs(across[0], n_cols, "cols")
        inv = chol_call(parity_order, own, other, inv, skip)
        for g in range(done, end + 1):
            raws += line_all_reduce(raw_call(*parts[g], hi, lo, line_parts[g]), "rows", n_rows)
        crosses.append(cross_call(inv, raws, skip))
        skip, done = sum(widths[: end + 1]), end + 1
    bh, bl = basis_call(inv, parts)
    sqs = []
    for c in crosses:
        own, other = gather_by_pairs(c[3], n_cols, "cols")
        sqs.append(sum(own[1:], own[0]) + jnp.sum(other, axis=0, keepdims=True))
    momentum_next = momentum_call(order, bh, bl, hi, lo, [c[1] for c in crosses], [c[2] for c in crosses])
    factor = momentum_prev.shape[0] * n_rows / rank**0.5
    update, q_next = update_call(order, bh, bl, [c[0] for c in crosses], sqs, factor)
    return momentum_next, q_next, update


def plain(n_rows, n_cols, momentum_prev, gradient, q_prev):
    high = lax.Precision.HIGHEST
    dot = functools.partial(lax.dot_general, precision=high, preferred_element_type=F32)
    momentum = 0.95 * momentum_prev + gradient.astype(F32)
    power = lax.psum_scatter(dot(momentum, q_prev, NN), "cols", scatter_dimension=0, tiled=True)
    power = lax.all_gather(power, "cols", axis=0, tiled=True)
    tn = (((0,), (0,)), ((), ()))
    raw, gram = lax.psum((dot(momentum, power, tn), dot(power, power, tn)), "rows")
    chol = jnp.linalg.cholesky(gram)
    solve = functools.partial(lax.linalg.triangular_solve, chol, left_side=False, lower=True, transpose_a=True)
    basis, cross = solve(power), solve(raw)
    q_next = cross / (jnp.sqrt(lax.psum(jnp.sum(cross * cross, axis=0), "cols")) + 1e-08)
    momentum_next = momentum - 0.5 * dot(basis, cross, NT)
    factor = momentum_prev.shape[0] * n_rows / jnp.sqrt(jnp.float32(q_prev.shape[1]))
    return momentum_next, q_next, (factor * dot(basis, q_next, NT)).astype(BF16)


def solution(mesh):
    n_rows, n_cols = mesh.shape["rows"], mesh.shape["cols"]

    def body(momentum_prev, gradient, q_prev):
        rows, cols = momentum_prev.shape
        block = rows // n_cols
        fits = (
            n_rows & (n_rows - 1) == 0
            and n_cols & (n_cols - 1) == 0
            and 4 <= n_cols <= CHUNK // 8
            and block % 128 == 0
            and cols % 128 == 0
            and q_prev.shape[1] % CHUNK == 0
        )
        return (fast if fits else plain)(n_rows, n_cols, momentum_prev, gradient, q_prev)

    in_specs = (P("rows", "cols"), P("rows", "cols"), P("cols", None))
    out_specs = (P("rows", "cols"), P("cols", None), P("rows", "cols"))
    return jax.shard_map(body, mesh=mesh, in_specs=in_specs, out_specs=out_specs, check_vma=False)
```

time: 532 us -> 244 us (0.46)
  waiting for transfers between devices: 214 us -> 64.8 us
  matrix products: 135 us -> 0 us
  other arithmetic: 123 us -> 12.4 us
  Pallas kernels: 0 us -> 76.9 us
  starting transfers between devices: 0.12 us -> 75.9 us
  between operations: 16.9 us -> 1.74 us
  local copies, waits for them, and re-layouts: 22 us -> 8 us
  blocking collectives: 14 us -> 0 us
    psum x1 -> x0, waiting for transfers between devices: 122 us -> none  [body(): raw_cross, gram = lax.psum((raw_part, partial_gram), 'rows')]
    another operation x17 -> x0, other arithmetic: 120 us -> none  [the longest x14 78.5 us: body(): chol = jnp.linalg.cholesky(gram)]
    dot_general x5 -> x0, matrix products: 95.1 us -> none  [the longest x1 31.3 us: body(): lax.dot_general(momentum, power, (((0,), (0,)), ((), ())), precision=high...]
    pallas_call x0 -> x14, Pallas kernels: none -> 76.9 us  [the longest x2 23.3 us: chol_call(): pl.pallas_call(functools.partial(chol_kernel, len(own), skip), in_specs=[...]
    ppermute x0 -> x55, starting transfers between devices: none -> 75.9 us  [the longest x6 18.6 us: fast(): lax.ppermute(gram, 'rows', [(i, i ^ m) for i in range(n_rows)])]
    ppermute x0 -> x55, waiting for transfers between devices: none -> 64.8 us  [the longest x6 19 us: fast(): s = lax.ppermute(k[n:] + r[n:], 'cols', perm)]
    reduce_scatter x1 -> x0, waiting for transfers between devices: 54.1 us -> none  [body(): lax.psum_scatter(jnp.dot(momentum, q_prev, precision=highest, preferred_e...]
    another operation x20 -> x0, matrix products: 39.4 us -> none  [the longest x7 21.2 us: body(): lax.linalg.triangular_solve(chol, power, left_side=False, lower=True, tra...]
  transfers between devices with their start and end apart: 3 -> 55, of which waited for: 3 -> 16; matrix products, arithmetic and copies ran while one was open for 0% -> 5% of each run, Pallas kernels for 0% -> 25%
where the time goes in v1:
time: 244 us; the launch traced here: 240 us
  Pallas kernels  76.9 us (32%)
  starting transfers between devices  75.9 us (31%)
  waiting for transfers between devices  64.8 us (27%)
  other arithmetic  12.4 us (5%)
  local copies, waits for them, and re-layouts  8 us (3%)
    pallas_call x2, Pallas kernels, chol_call(): pl.pallas_call(functools.partial(chol_kernel, len(own), skip), in_specs=[...  23.3 us
    ppermute x6, waiting for transfers between devices, fast(): s = lax.ppermute(k[n:] + r[n:], 'cols', perm)  19 us
    ppermute x6, starting transfers between devices, fast(): lax.ppermute(gram, 'rows', [(i, i ^ m) for i in range(n_rows)])  18.6 us
    ppermute x12, starting transfers between devices, gather_by_pairs(): lax.ppermute(x, axis, [(j, j ^ m) for j in range(n)])  13.2 us
    ppermute x5, waiting for transfers between devices, line_all_reduce(): r = lax.ppermute(x, axis, [(s + 1, s), (n - 2 - s, n - 1 - s)])  12.2 us
    ppermute x6, waiting for transfers between devices, fast(): x = jnp.concatenate([x, lax.ppermute(x, 'cols', perm)], axis=0)  11.9 us
    ppermute x5, waiting for transfers between devices, line_all_reduce(): x = x + lax.ppermute(x, axis, [(s, s + 1), (n - 1 - s, n - 2 - s)])  11.9 us
    ppermute x5, starting transfers between devices, line_all_reduce(): x = x + lax.ppermute(x, axis, [(s, s + 1), (n - 1 - s, n - 2 - s)])  11.9 us
  transfers between devices with their start and end apart: 55, of which 16 were waited for; matrix products, arithmetic and copies ran while one was open for 5% of the time, Pallas kernels for 25%

profile of v1, /device:TPU:0, one launch (start us, length us, event | category | flops | bytes accessed | tf_op | source)
XLA Modules:
  0.0 239.7 jit_solution(4805523542815986662)
XLA Ops:
  1.3 2.2 copy-done.6
  5.1 6.6 %momentum_and_power.1 = (bf16[2048,1024]{1,0:T(8,128)(2,1)S(1)}, bf16[2048,1024]{1,0:T(8,128)(2,1)S(1)}, f32[4,128,256]{2,1,0:T(8,128)S(1)}, f32[4,128,256]{2,1,0:T(8,128)S(1)}) custom-call(s32[8]{0:T(128)S(1)} %fusion.3.order_ref, f32[2048,1024]{1,0:T(8,128)} %mp_ref.1, bf16[2048,1024]{1,0:T(8,128)(2,1)S(1)} %copy-done.6, f32[1024,512]{1,0:T(8,128)S(1)} %copy-done.7), custom_call_target="tpu_custom_call" | custom-call | flops 1610612736 | bytes 12582912 | tf_op jit(solution)/shard_map/momentum_and_power/pallas_call | solution.py:144
  13.8 2.9 %collective-permute-start.1 = (f32[2,128,256]{2,1,0:T(8,128)S(1)}, f32[2,128,256]{2,1,0:T(8,128)S(1)}, u32[]{:S(2)}, u32[]{:S(2)}) collective-permute-start(f32[2,128,256]{2,1,0:T(8,128)S(1)} %get-tuple-element.58), channel_id=1, source_target_pairs={{0,2},{1,5},{2,0},{3,7},{4,6},{5,1},{6,4},{7,3},{8,10},{9,13},{10,... | collective-permute-start | bytes 786440 | tf_op jit(solution)/shard_map/ppermute | solution.py:539
  16.7 7.2 %power.1 = (f32[4,128,256]{2,1,0:T(8,128)S(1)}, f32[4,256,256]{2,1,0:T(8,128)S(1)}, f32[4,128,256]{2,1,0:T(8,128)S(1)}, f32[4,256,256]{2,1,0:T(8,128)S(1)}) custom-call(bf16[2048,1024]{1,0:T(8,128)(2,1)S(1)} %get-tuple-element.30.hi_ref, bf16[2048,1024]{1,0:T(8,128)(2,1)S(1)} %get-tuple-element.31.lo_ref, f32[1024,512]{1,0:T(8,128)S(1)} %copy-done.7), custom_call_target="tpu_custom_call" | custom-call | flops 4831838208 | bytes 8388608 | tf_op jit(solution)/shard_map/power/pallas_call | solution.py:180
  25.7 3.4 %collective-permute-done.2 = f32[1,128,256]{2,1,0:T(8,128)S(1)} collective-permute-done((f32[1,128,256]{2,1,0:T(8,128)S(1)}, f32[1,128,256]{2,1,0:T(8,128)S(1)}, u32[]{:S(2)}, u32[]{:S(2)}) %collective-permute-start.2) | collective-permute-done | bytes 131104 | tf_op jit(solution)/shard_map/ppermute | solution.py:539
  30.6 5.0 %collective-permute-done.7 = f32[2,128,256]{2,1,0:T(8,128)S(1)} collective-permute-done((f32[2,128,256]{2,1,0:T(8,128)S(1)}, f32[2,128,256]{2,1,0:T(8,128)S(1)}, u32[]{:S(2)}, u32[]{:S(2)}) %collective-permute-start.7) | collective-permute-done | bytes 262176 | tf_op jit(solution)/shard_map/ppermute | solution.py:539
  37.3 3.4 %collective-permute-done.8 = f32[1,128,256]{2,1,0:T(8,128)S(1)} collective-permute-done((f32[1,128,256]{2,1,0:T(8,128)S(1)}, f32[1,128,256]{2,1,0:T(8,128)S(1)}, u32[]{:S(2)}, u32[]{:S(2)}) %collective-permute-start.8) | collective-permute-done | bytes 131104 | tf_op jit(solution)/shard_map/ppermute | solution.py:539
  43.0 7.1 %collective-permute-done.13 = f32[2,256,256]{2,1,0:T(8,128)S(1)} collective-permute-done((f32[2,256,256]{2,1,0:T(8,128)S(1)}, f32[2,256,256]{2,1,0:T(8,128)S(1)}, u32[]{:S(2)}, u32[]{:S(2)}) %collective-permute-start.13) | collective-permute-done | bytes 524320 | tf_op jit(solution)/shard_map/ppermute | solution.py:539
  53.7 7.2 %collective-permute-done.9 = f32[1,128,256]{2,1,0:T(8,128)S(1)} collective-permute-done((f32[1,128,256]{2,1,0:T(8,128)S(1)}, f32[1,128,256]{2,1,0:T(8,128)S(1)}, u32[]{:S(2)}, u32[]{:S(2)}) %collective-permute-start.9) | collective-permute-done | bytes 131104 | tf_op jit(solution)/shard_map/ppermute | solution.py:543
  63.4 4.0 %collective-permute-done.10 = f32[2,128,256]{2,1,0:T(8,128)S(1)} collective-permute-done((f32[2,128,256]{2,1,0:T(8,128)S(1)}, f32[2,128,256]{2,1,0:T(8,128)S(1)}, u32[]{:S(2)}, u32[]{:S(2)}) %collective-permute-start.10) | collective-permute-done | bytes 262176 | tf_op jit(solution)/shard_map/ppermute | solution.py:543
  71.4 3.5 %collective-permute-start.32 = (f32[128,1024]{1,0:T(8,128)S(1)}, f32[128,1024]{1,0:T(8,128)S(1)}, u32[]{:S(2)}, u32[]{:S(2)}) collective-permute-start(f32[128,1024]{1,0:T(8,128)S(1)} %raw.3), channel_id=1, source_target_pairs={{0,8},{24,16},{1,9},{25,17},{2,10},{26,18},{3,11},{27,19},{4,12},{... | collective-permute-start | bytes 1572872 | tf_op jit(solution)/shard_map/ppermute | solution.py:91
  78.5 1.8 gram.3
  80.3 2.8 %collective-permute-start.27 = (f32[32,256]{1,0:T(8,128)S(1)}, f32[32,256]{1,0:T(8,128)S(1)}, u32[]{:S(2)}, u32[]{:S(2)}) collective-permute-start(f32[32,256]{1,0:T(8,128)S(1)} %gram.3), channel_id=1, source_target_pairs={{0,24},{8,16},{16,8},{24,0},{1,25},{9,17},{17,9},{25,1},{2,26},{10... | collective-permute-start | bytes 98312 | tf_op jit(solution)/shard_map/ppermute | solution.py:548
  83.2 4.0 %collective-permute-done.32 = f32[128,1024]{1,0:T(8,128)S(1)} collective-permute-done((f32[128,1024]{1,0:T(8,128)S(1)}, f32[128,1024]{1,0:T(8,128)S(1)}, u32[]{:S(2)}, u32[]{:S(2)}) %collective-permute-start.32) | collective-permute-done | bytes 524320 | tf_op jit(solution)/shard_map/ppermute | solution.py:91
  87.2 2.5 %collective-permute-start.25 = (f32[32,256]{1,0:T(8,128)S(1)}, f32[32,256]{1,0:T(8,128)S(1)}, u32[]{:S(2)}, u32[]{:S(2)}) collective-permute-start(f32[32,256]{1,0:T(8,128)S(1)} %gram.3), channel_id=1, source_target_pairs={{0,8},{8,0},{16,24},{24,16},{1,9},{9,1},{17,25},{25,17},{2,10},{10... | collective-permute-start | bytes 98312 | tf_op jit(solution)/shard_map/ppermute | solution.py:548
  90.5 7.9 %collective-permute-done.35 = f32[128,1024]{1,0:T(8,128)S(1)} collective-permute-done((f32[128,1024]{1,0:T(8,128)S(1)}, f32[128,1024]{1,0:T(8,128)S(1)}, u32[]{:S(2)}, u32[]{:S(2)}) %collective-permute-start.35) | collective-permute-done | bytes 524320 | tf_op jit(solution)/shard_map/ppermute | solution.py:91
  105.2 2.9 %collective-permute-done.30.refs_3_ = f32[32,256]{1,0:T(8,128)S(1)} collective-permute-done((f32[32,256]{1,0:T(8,128)S(1)}, f32[32,256]{1,0:T(8,128)S(1)}, u32[]{:S(2)}, u32[]{:S(2)}) %collective-permute-start.30) | collective-permute-done | bytes 32800 | tf_op jit(solution)/shard_map/ppermute | solution.py:81
  108.6 3.4 %collective-permute-done.28.refs_1_ = f32[32,256]{1,0:T(8,128)S(1)} collective-permute-done((f32[32,256]{1,0:T(8,128)S(1)}, f32[32,256]{1,0:T(8,128)S(1)}, u32[]{:S(2)}, u32[]{:S(2)}) %collective-permute-start.28) | collective-permute-done | bytes 32800 | tf_op jit(solution)/shard_map/ppermute | solution.py:81
  117.6 5.4 %gram.2 = f32[32,512]{1,0:T(8,128)S(1)} custom-call(s32[1]{0:T(128)} %bitcast.me_ref, f32[4,128,256]{2,1,0:T(8,128)S(1)} %pad_maximum_fusion.1.refs_0_.pa_ref, f32[4,128,256]{2,1,0:T(8,128)S(1)} %collective-permute-done.5.refs_1_.pb_ref, f32[4,128,256]{2,1,0:T(8,128)S(1)} %pad_maximum_fusion.2.refs_2_.pa_ref, ...), custom_call_target="tpu_custom_call" | custom-call | flops 4000000000 | bytes 6291456 | tf_op jit(solution)/shard_map/gram/pallas_call | solution.py:254
  124.5 11.5 %collective-permute-start.19 = (f32[32,512]{1,0:T(8,128)S(1)}, f32[32,512]{1,0:T(8,128)S(1)}, u32[]{:S(2)}, u32[]{:S(2)}) collective-permute-start(f32[32,512]{1,0:T(8,128)S(1)} %gram.2), channel_id=1, source_target_pairs={{0,16},{8,24},{16,0},{24,8},{1,17},{9,25},{17,1},{25,9},{2,18},{10... | collective-permute-start | bytes 196616 | tf_op jit(solution)/shard_map/ppermute | solution.py:548
  136.1 4.6 %raw.5 = (f32[128,1024]{1,0:T(8,128)S(1)}, f32[64,1024]{1,0:T(8,128)S(1)}, f32[64,1024]{1,0:T(8,128)S(1)}) custom-call(f32[4,256,256]{2,1,0:T(8,128)S(1)} %pad_maximum_fusion.refs_4_.pa_ref, f32[4,256,256]{2,1,0:T(8,128)} %collective-permute-done.17.refs_5_.pb_ref, bf16[2048,1024]{1,0:T(8,128)(2,1)S(1)} %copy-done.1, bf16[2048,1024]{1,0:T(8,128)(2,1)S(1)} %copy-done.4), custom_call_target="tpu_custom_call" | custom-call | flops 3221225472 | bytes 8388608 | tf_op jit(solution)/shard_map/raw/pallas_call | solution.py:211
  140.9 4.2 %collective-permute-start.38 = (f32[128,1024]{1,0:T(8,128)S(1)}, f32[128,1024]{1,0:T(8,128)S(1)}, u32[]{:S(2)}, u32[]{:S(2)}) collective-permute-start(f32[128,1024]{1,0:T(8,128)S(1)} %get-tuple-element.41), channel_id=1, source_target_pairs={{0,8},{24,16},{1,9},{25,17},{2,10},{26,18},{3,11},{27,19},{4,12},{... | collective-permute-start | bytes 1572872 | tf_op jit(solution)/shard_map/ppermute | solution.py:91
  145.1 10.6 %chol.2.refs_5_.inv_ref = f32[256,256]{1,0:T(8,128)S(1)} custom-call(s32[8]{0:T(128)S(1)} %broadcast_xor_fusion.order_ref, f32[32,256]{1,0:T(8,128)S(1)} %add_add_fusion.1.refs_0_, f32[32,256]{1,0:T(8,128)S(1)} %collective-permute-done.28.refs_1_, f32[32,256]{1,0:T(8,128)S(1)} %collective-permute-done.29.refs_2_, ...), custom_call_target="tpu_custom_call" | custom-call | flops 12000000000 | bytes 524288 | tf_op jit(solution)/shard_map/chol/pallas_call | solution.py:350
  161.0 2.0 collective-permute-start.21
  166.9 2.0 collective-permute-start.47
  183.7 12.7 %chol.3.inv_ref = f32[512,512]{1,0:T(8,128)S(1)} custom-call(s32[8]{0:T(128)S(1)} %broadcast_xor_fusion.order_ref, f32[32,512]{1,0:T(8,128)S(1)} %add_add_fusion.refs_0_, f32[32,512]{1,0:T(8,128)S(1)} %collective-permute-done.21.refs_1_, f32[32,512]{1,0:T(8,128)S(1)} %collective-permute-done.22.refs_2_, f32[32,512]{1,0:T(8,128)S(1)} %collective-permute-done.23.refs_3_, ...), custom_call_target="tpu_custom_call" | custom-call | flops 12000000000 | bytes 2097152 | tf_op jit(solution)/shard_map/chol/pallas_call | solution.py:350
  196.5 2.0 collective-permute-done.46
  198.5 10.2 %collective-permute-done.40 = f32[128,1024]{1,0:T(8,128)S(1)} collective-permute-done((f32[128,1024]{1,0:T(8,128)S(1)}, f32[128,1024]{1,0:T(8,128)S(1)}, u32[]{:S(2)}, u32[]{:S(2)}) %collective-permute-start.40) | collective-permute-done | bytes 524320 | tf_op jit(solution)/shard_map/ppermute | solution.py:94
  211.6 2.0 collective-permute-start.51
  213.6 5.1 %basis.1 = (bf16[2048,512]{1,0:T(8,128)(2,1)S(1)}, bf16[2048,512]{1,0:T(8,128)(2,1)S(1)}) custom-call(f32[512,512]{1,0:T(8,128)S(1)} %chol.3.inv_ref, f32[4,128,256]{2,1,0:T(8,128)S(1)} %pad_maximum_fusion.1.refs_0_.pa_ref, f32[4,128,256]{2,1,0:T(8,128)S(1)} %copy-done.9, f32[4,128,256]{2,1,0:T(8,128)S(1)} %pad_maximum_fusion.2.refs_2_.pa_ref, ...), custom_call_target="tpu_custom_call" | custom-call | flops 3221225472 | bytes 8388608 | tf_op jit(solution)/shard_map/basis/pallas_call | solution.py:377
  218.9 8.4 %momentum_next.1 = f32[2048,1024]{1,0:T(8,128)} custom-call(s32[8]{0:T(128)S(1)} %fusion.3.order_ref, bf16[2048,512]{1,0:T(8,128)(2,1)S(1)} %get-tuple-element.38.bh_ref, bf16[2048,512]{1,0:T(8,128)(2,1)S(1)} %get-tuple-element.39.bl_ref, bf16[2048,1024]{1,0:T(8,128)(2,1)S(1)} %copy-done.2, bf16[2048,1024]{1,0:T(8,128)(2,1)S(1)} %copy-done.5, ...), custom_call_target="tpu_custom_call" | custom-call | flops 6442450944 | bytes 16777216 | tf_op jit(solution)/shard_map/momentum_next/pallas_call | solution.py:442
  230.6 8.8 %update.1 = (bf16[2048,1024]{1,0:T(8,128)(2,1)}, f32[1024,512]{1,0:T(8,128)}) custom-call(s32[8]{0:T(128)S(1)} %fusion.3.order_ref, bf16[2048,512]{1,0:T(8,128)(2,1)S(1)} %copy-done.23, bf16[2048,512]{1,0:T(8,128)(2,1)S(1)} %copy-done.25, f32[256,1024]{1,0:T(8,128)S(1)} %copy-done.15, f32[256,1024]{1,0:T(8,128)S(1)} %copy-done.13, ...), custom_call_target="tpu_custom_call" | custom-call | flops 6442450944 | bytes 16777216 | tf_op jit(solution)/shard_map/update/pallas_call | solution.py:484
  (188 shorter events, 70.5 us)
Async XLA Ops:
  13.8 10.2 %collective-permute-start.1 = (f32[2,128,256]{2,1,0:T(8,128)S(1)}, f32[2,128,256]{2,1,0:T(8,128)S(1)}, u32[]{:S(2)}, u32[]{:S(2)}) collective-permute-start(f32[2,128,256]{2,1,0:T(8,128)S(1)} %get-tuple-element.58), channel_id=1, source_target_pairs={{0,2},{1,5},{2,0},{3,7},{4,6},{5,1},{6,4},{7,3},{8,10},{9,13},{10,... | collective-permute-start | bytes 786440 | tf_op jit(solution)/shard_map/ppermute | solution.py:539
  25.7 15.1 %collective-permute-start.12 = (f32[4,256,256]{2,1,0:T(8,128)S(1)}, f32[4,256,256]{2,1,0:T(8,128)S(1)}, u32[]{:S(2)}, u32[]{:S(2)}) collective-permute-start(f32[4,256,256]{2,1,0:T(8,128)S(1)} %get-tuple-element.36), channel_id=1, source_target_pairs={{0,1},{1,0},{2,3},{3,2},{4,5},{5,4},{6,7},{7,6},{8,9},{9,8},{10,11... | collective-permute-start | bytes 3145736 | tf_op jit(solution)/shard_map/ppermute | solution.py:534
  40.9 9.2 %collective-permute-start.13 = (f32[2,256,256]{2,1,0:T(8,128)S(1)}, f32[2,256,256]{2,1,0:T(8,128)S(1)}, u32[]{:S(2)}, u32[]{:S(2)}) collective-permute-start(f32[2,256,256]{2,1,0:T(8,128)S(1)} %get-tuple-element.54), channel_id=1, source_target_pairs={{0,2},{1,5},{2,0},{3,7},{4,6},{5,1},{6,4},{7,3},{8,10},{9,13},{10,... | collective-permute-start | bytes 1572872 | tf_op jit(solution)/shard_map/ppermute | solution.py:539
  42.3 10.0 %collective-permute-start.3 = (f32[1,128,256]{2,1,0:T(8,128)S(1)}, f32[1,128,256]{2,1,0:T(8,128)S(1)}, u32[]{:S(2)}, u32[]{:S(2)}) collective-permute-start(f32[1,128,256]{2,1,0:T(8,128)S(1)} %fusion.2), channel_id=1, source_target_pairs={{0,4},{1,3},{2,6},{3,1},{4,0},{5,7},{6,2},{7,5},{8,12},{9,11},{10,... | collective-permute-start | bytes 393224 | tf_op jit(solution)/shard_map/ppermute | solution.py:543
  50.2 11.6 %collective-permute-start.14 = (f32[1,256,256]{2,1,0:T(8,128)S(1)}, f32[1,256,256]{2,1,0:T(8,128)S(1)}, u32[]{:S(2)}, u32[]{:S(2)}) collective-permute-start(f32[1,256,256]{2,1,0:T(8,128)S(1)} %slice_add_fusion.2), channel_id=1, source_target_pairs={{0,4},{1,3},{2,6},{3,1},{4,0},{5,7},{6,2},{7,5},{8,12},{9,11},{10,... | collective-permute-start | bytes 786440 | tf_op jit(solution)/shard_map/ppermute | solution.py:539
  51.8 9.1 %collective-permute-start.9 = (f32[1,128,256]{2,1,0:T(8,128)S(1)}, f32[1,128,256]{2,1,0:T(8,128)S(1)}, u32[]{:S(2)}, u32[]{:S(2)}) collective-permute-start(f32[1,128,256]{2,1,0:T(8,128)S(1)} %fusion.1), channel_id=1, source_target_pairs={{0,4},{1,3},{2,6},{3,1},{4,0},{5,7},{6,2},{7,5},{8,12},{9,11},{10,... | collective-permute-start | bytes 393224 | tf_op jit(solution)/shard_map/ppermute | solution.py:543
  52.3 11.0 %collective-permute-start.4 = (f32[2,128,256]{2,1,0:T(8,128)S(1)}, f32[2,128,256]{2,1,0:T(8,128)S(1)}, u32[]{:S(2)}, u32[]{:S(2)}) collective-permute-start(f32[2,128,256]{2,1,0:T(8,128)S(1)} %pad_maximum_fusion.4), channel_id=1, source_target_pairs={{0,2},{1,5},{2,0},{3,7},{4,6},{5,1},{6,4},{7,3},{8,10},{9,13},{10,... | collective-permute-start | bytes 786440 | tf_op jit(solution)/shard_map/ppermute | solution.py:543
  68.3 10.0 %collective-permute-start.16 = (f32[2,256,256]{2,1,0:T(8,128)S(1)}, f32[2,256,256]{2,1,0:T(8,128)S(1)}, u32[]{:S(2)}, u32[]{:S(2)}) collective-permute-start(f32[2,256,256]{2,1,0:T(8,128)S(1)} %pad_maximum_fusion.3), channel_id=1, source_target_pairs={{0,2},{1,5},{2,0},{3,7},{4,6},{5,1},{6,4},{7,3},{8,10},{9,13},{10,... | collective-permute-start | bytes 1572872 | tf_op jit(solution)/shard_map/ppermute | solution.py:543
  71.4 15.8 %collective-permute-start.32 = (f32[128,1024]{1,0:T(8,128)S(1)}, f32[128,1024]{1,0:T(8,128)S(1)}, u32[]{:S(2)}, u32[]{:S(2)}) collective-permute-start(f32[128,1024]{1,0:T(8,128)S(1)} %raw.3), channel_id=1, source_target_pairs={{0,8},{24,16},{1,9},{25,17},{2,10},{26,18},{3,11},{27,19},{4,12},{... | collective-permute-start | bytes 1572872 | tf_op jit(solution)/shard_map/ppermute | solution.py:91
  76.8 21.6 %collective-permute-start.35 = (f32[128,1024]{1,0:T(8,128)S(1)}, f32[128,1024]{1,0:T(8,128)S(1)}, u32[]{:S(2)}, u32[]{:S(2)}) collective-permute-start(f32[128,1024]{1,0:T(8,128)S(1)} %raw.4), channel_id=1, source_target_pairs={{0,8},{24,16},{1,9},{25,17},{2,10},{26,18},{3,11},{27,19},{4,12},{... | collective-permute-start | bytes 1572872 | tf_op jit(solution)/shard_map/ppermute | solution.py:91
  78.4 39.1 %collective-permute-start.17 = (f32[4,256,256]{2,1,0:T(8,128)S(1)}, f32[4,256,256]{2,1,0:T(8,128)}, u32[]{:S(2)}, u32[]{:S(2)}) collective-permute-start(f32[4,256,256]{2,1,0:T(8,128)S(1)} %pad_maximum_fusion.refs_4_.pa_ref), channel_id=1, source_target_pairs={{0,1},{1,0},{2,3},{3,2},{4,5},{5,4},{6,7},{7,6},{8,9},{9,8},{10,11... | collective-permute-start | bytes 3145736 | tf_op jit(solution)/shard_map/ppermute | solution.py:544
  80.3 21.4 %collective-permute-start.27 = (f32[32,256]{1,0:T(8,128)S(1)}, f32[32,256]{1,0:T(8,128)S(1)}, u32[]{:S(2)}, u32[]{:S(2)}) collective-permute-start(f32[32,256]{1,0:T(8,128)S(1)} %gram.3), channel_id=1, source_target_pairs={{0,24},{8,16},{16,8},{24,0},{1,25},{9,17},{17,9},{25,1},{2,26},{10... | collective-permute-start | bytes 98312 | tf_op jit(solution)/shard_map/ppermute | solution.py:548
  83.2 20.0 %collective-permute-start.26 = (f32[32,256]{1,0:T(8,128)S(1)}, f32[32,256]{1,0:T(8,128)S(1)}, u32[]{:S(2)}, u32[]{:S(2)}) collective-permute-start(f32[32,256]{1,0:T(8,128)S(1)} %gram.3), channel_id=1, source_target_pairs={{0,16},{8,24},{16,0},{24,8},{1,17},{9,25},{17,1},{25,9},{2,18},{10... | collective-permute-start | bytes 98312 | tf_op jit(solution)/shard_map/ppermute | solution.py:548
  87.2 16.0 %collective-permute-start.25 = (f32[32,256]{1,0:T(8,128)S(1)}, f32[32,256]{1,0:T(8,128)S(1)}, u32[]{:S(2)}, u32[]{:S(2)}) collective-permute-start(f32[32,256]{1,0:T(8,128)S(1)} %gram.3), channel_id=1, source_target_pairs={{0,8},{8,0},{16,24},{24,16},{1,9},{9,1},{17,25},{25,17},{2,10},{10... | collective-permute-start | bytes 98312 | tf_op jit(solution)/shard_map/ppermute | solution.py:548
  98.4 13.7 %collective-permute-start.33 = (f32[128,1024]{1,0:T(8,128)}, f32[128,1024]{1,0:T(8,128)}, u32[]{:S(2)}, u32[]{:S(2)}) collective-permute-start(f32[128,1024]{1,0:T(8,128)} %add.143), channel_id=1, source_target_pairs={{8,16},{16,8},{9,17},{17,9},{10,18},{18,10},{11,19},{19,11},{12,20... | collective-permute-start | bytes 1572872 | tf_op jit(solution)/shard_map/ppermute | solution.py:92
  101.7 13.0 %collective-permute-start.36 = (f32[128,1024]{1,0:T(8,128)}, f32[128,1024]{1,0:T(8,128)}, u32[]{:S(2)}, u32[]{:S(2)}) collective-permute-start(f32[128,1024]{1,0:T(8,128)} %add.145), channel_id=1, source_target_pairs={{8,16},{16,8},{9,17},{17,9},{10,18},{18,10},{11,19},{19,11},{12,20... | collective-permute-start | bytes 1572872 | tf_op jit(solution)/shard_map/ppermute | solution.py:92
  112.0 28.7 %collective-permute-start.31 = (f32[128,256]{1,0:T(8,128)S(1)}, f32[128,256]{1,0:T(8,128)S(1)}, u32[]{:S(2)}, u32[]{:S(2)}) collective-permute-start(f32[128,256]{1,0:T(8,128)S(1)} %pad_maximum_fusion.7), channel_id=1, source_target_pairs={{0,1},{1,0},{2,3},{3,2},{4,5},{5,4},{6,7},{7,6},{8,9},{9,8},{10,11... | collective-permute-start | bytes 393224 | tf_op jit(solution)/shard_map/ppermute | solution.py:82
  113.4 42.5 %collective-permute-start.34 = (f32[128,1024]{1,0:T(8,128)S(1)}, f32[128,1024]{1,0:T(8,128)S(1)}, u32[]{:S(2)}, u32[]{:S(2)}) collective-permute-start(f32[128,1024]{1,0:T(8,128)S(1)} %add.144), channel_id=1, source_target_pairs={{8,0},{16,24},{9,1},{17,25},{10,2},{18,26},{11,3},{19,27},{12,4},{... | collective-permute-start | bytes 1572872 | tf_op jit(solution)/shard_map/ppermute | solution.py:94
  116.0 45.0 %collective-permute-start.37 = (f32[128,1024]{1,0:T(8,128)S(1)}, f32[128,1024]{1,0:T(8,128)S(1)}, u32[]{:S(2)}, u32[]{:S(2)}) collective-permute-start(f32[128,1024]{1,0:T(8,128)S(1)} %add.146), channel_id=1, source_target_pairs={{8,0},{16,24},{9,1},{17,25},{10,2},{18,26},{11,3},{19,27},{12,4},{... | collective-permute-start | bytes 1572872 | tf_op jit(solution)/shard_map/ppermute | solution.py:94
  123.0 17.9 %collective-permute-start.20 = (f32[32,512]{1,0:T(8,128)S(1)}, f32[32,512]{1,0:T(8,128)S(1)}, u32[]{:S(2)}, u32[]{:S(2)}) collective-permute-start(f32[32,512]{1,0:T(8,128)S(1)} %gram.2), channel_id=1, source_target_pairs={{0,24},{8,16},{16,8},{24,0},{1,25},{9,17},{17,9},{25,1},{2,26},{10... | collective-permute-start | bytes 196616 | tf_op jit(solution)/shard_map/ppermute | solution.py:548
  124.5 31.2 %collective-permute-start.19 = (f32[32,512]{1,0:T(8,128)S(1)}, f32[32,512]{1,0:T(8,128)S(1)}, u32[]{:S(2)}, u32[]{:S(2)}) collective-permute-start(f32[32,512]{1,0:T(8,128)S(1)} %gram.2), channel_id=1, source_target_pairs={{0,16},{8,24},{16,0},{24,8},{1,17},{9,25},{17,1},{25,9},{2,18},{10... | collective-permute-start | bytes 196616 | tf_op jit(solution)/shard_map/ppermute | solution.py:548
  140.7 15.0 %collective-permute-start.18 = (f32[32,512]{1,0:T(8,128)S(1)}, f32[32,512]{1,0:T(8,128)S(1)}, u32[]{:S(2)}, u32[]{:S(2)}) collective-permute-start(f32[32,512]{1,0:T(8,128)S(1)} %gram.2), channel_id=1, source_target_pairs={{0,8},{8,0},{16,24},{24,16},{1,9},{9,1},{17,25},{25,17},{2,10},{10... | collective-permute-start | bytes 196616 | tf_op jit(solution)/shard_map/ppermute | solution.py:548
  140.9 17.7 %collective-permute-start.38 = (f32[128,1024]{1,0:T(8,128)S(1)}, f32[128,1024]{1,0:T(8,128)S(1)}, u32[]{:S(2)}, u32[]{:S(2)}) collective-permute-start(f32[128,1024]{1,0:T(8,128)S(1)} %get-tuple-element.41), channel_id=1, source_target_pairs={{0,8},{24,16},{1,9},{25,17},{2,10},{26,18},{3,11},{27,19},{4,12},{... | collective-permute-start | bytes 1572872 | tf_op jit(solution)/shard_map/ppermute | solution.py:91
  155.9 11.0 %collective-permute-start.41 = (f32[64,1024]{1,0:T(8,128)S(1)}, f32[64,1024]{1,0:T(8,128)S(1)}, u32[]{:S(2)}, u32[]{:S(2)}) collective-permute-start(f32[64,1024]{1,0:T(8,128)S(1)} %get-tuple-element.42), channel_id=1, source_target_pairs={{0,8},{24,16},{1,9},{25,17},{2,10},{26,18},{3,11},{27,19},{4,12},{... | collective-permute-start | bytes 786440 | tf_op jit(solution)/shard_map/ppermute | solution.py:91
  157.2 13.1 %collective-permute-start.44 = (f32[64,1024]{1,0:T(8,128)S(1)}, f32[64,1024]{1,0:T(8,128)S(1)}, u32[]{:S(2)}, u32[]{:S(2)}) collective-permute-start(f32[64,1024]{1,0:T(8,128)S(1)} %get-tuple-element.43), channel_id=1, source_target_pairs={{0,8},{24,16},{1,9},{25,17},{2,10},{26,18},{3,11},{27,19},{4,12},{... | collective-permute-start | bytes 786440 | tf_op jit(solution)/shard_map/ppermute | solution.py:91
  163.0 17.0 %collective-permute-start.39 = (f32[128,1024]{1,0:T(8,128)}, f32[128,1024]{1,0:T(8,128)}, u32[]{:S(2)}, u32[]{:S(2)}) collective-permute-start(f32[128,1024]{1,0:T(8,128)} %add.147), channel_id=1, source_target_pairs={{8,16},{16,8},{9,17},{17,9},{10,18},{18,10},{11,19},{19,11},{12,20... | collective-permute-start | bytes 1572872 | tf_op jit(solution)/shard_map/ppermute | solution.py:92
  170.3 12.4 %collective-permute-start.24 = (f32[128,512]{1,0:T(8,128)}, f32[128,512]{1,0:T(8,128)}, u32[]{:S(2)}, u32[]{:S(2)}) collective-permute-start(f32[128,512]{1,0:T(8,128)} %pad_maximum_fusion.6), channel_id=1, source_target_pairs={{0,1},{1,0},{2,3},{3,2},{4,5},{5,4},{6,7},{7,6},{8,9},{9,8},{10,11... | collective-permute-start | bytes 786440 | tf_op jit(solution)/shard_map/ppermute | solution.py:82
  176.3 20.1 %collective-permute-start.43 = (f32[64,1024]{1,0:T(8,128)S(1)}, f32[64,1024]{1,0:T(8,128)S(1)}, u32[]{:S(2)}, u32[]{:S(2)}) collective-permute-start(f32[64,1024]{1,0:T(8,128)S(1)} %add.150), channel_id=1, source_target_pairs={{8,0},{16,24},{9,1},{17,25},{10,2},{18,26},{11,3},{19,27},{12,4},{... | collective-permute-start | bytes 786440 | tf_op jit(solution)/shard_map/ppermute | solution.py:94
  178.7 19.8 %collective-permute-start.46 = (f32[64,1024]{1,0:T(8,128)S(1)}, f32[64,1024]{1,0:T(8,128)S(1)}, u32[]{:S(2)}, u32[]{:S(2)}) collective-permute-start(f32[64,1024]{1,0:T(8,128)S(1)} %add.152), channel_id=1, source_target_pairs={{8,0},{16,24},{9,1},{17,25},{10,2},{18,26},{11,3},{19,27},{12,4},{... | collective-permute-start | bytes 786440 | tf_op jit(solution)/shard_map/ppermute | solution.py:94
  181.3 27.5 %collective-permute-start.40 = (f32[128,1024]{1,0:T(8,128)S(1)}, f32[128,1024]{1,0:T(8,128)S(1)}, u32[]{:S(2)}, u32[]{:S(2)}) collective-permute-start(f32[128,1024]{1,0:T(8,128)S(1)} %add.148), channel_id=1, source_target_pairs={{8,0},{16,24},{9,1},{17,25},{10,2},{18,26},{11,3},{19,27},{12,4},{... | collective-permute-start | bytes 1572872 | tf_op jit(solution)/shard_map/ppermute | solution.py:94
  210.0 8.7 %collective-permute-start.53 = (f32[1,256]{1,0:T(1,128)S(1)}, f32[1,256]{1,0:T(1,128)S(1)}, u32[]{:S(2)}, u32[]{:S(2)}) collective-permute-start(f32[1,256]{1,0:T(1,128)S(1)} %get-tuple-element.50), channel_id=1, source_target_pairs={{0,6},{1,7},{2,4},{3,5},{4,2},{5,3},{6,0},{7,1},{8,14},{9,15},{10,... | collective-permute-start | bytes 3080 | tf_op jit(solution)/shard_map/ppermute | solution.py:81
  218.8 8.6 %collective-permute-start.54 = (f32[4,256]{1,0:T(4,128)S(1)}, f32[4,256]{1,0:T(4,128)S(1)}, u32[]{:S(2)}, u32[]{:S(2)}) collective-permute-start(f32[4,256]{1,0:T(4,128)S(1)} %pad_maximum_fusion.9), channel_id=1, source_target_pairs={{0,1},{1,0},{2,3},{3,2},{4,5},{5,4},{6,7},{7,6},{8,9},{9,8},{10,11... | collective-permute-start | bytes 12296 | tf_op jit(solution)/shard_map/ppermute | solution.py:82
  (50 other events, 578.2 us)
